TPU v7x, 32 devices: a whole 2x2x4 slice. The times are simulated.
32 devices in a mesh: dir: 4 (over x, core), bond: 8 (over z, y).
Axes of the slice: x: 2, y: 2, z: 4, core: 2. Of those that a mesh axis runs over, the one named last changes fastest.
Arguments:
- corner_mat: bfloat16 [4, 8192, 8192], P('dir', 'bond'), may hold values from -0.0625 to 0.0625
- edge_mat: bfloat16 [4, 32768, 8192], P('dir', 'bond'), may hold values from -0.0625 to 0.0625
- edge_panel: bfloat16 [4, 8192, 512], P('dir', 'bond'), may hold values from -6 to 6
- vertex_weights: float32 [4, 4, 4], replicated, may hold values from -3 to 3
- projector: bfloat16 [4, 512, 256], P('dir'), may hold values from -0.25 to 0.25
- edge_projector: bfloat16 [4, 8192, 256], P('dir', 'bond'), may hold values from -0.09375 to 0.09375
Outputs:
- new_corner: bfloat16 [4, 32768, 256], P('dir', 'bond')
- gram: float32 [4, 256, 256], P('dir', 'bond')
- new_edge: bfloat16 [4, 256, 512], P('dir', 'bond')
All inputs are finite; a program needn't handle non-finite values.
Results may differ from a plain program's by a relative error of at most 0.0065.
Values may be sent and summed in bfloat16 or wider, within the bound.
A program may use at most 256 MiB of HBM per device.

v0:
```python
import jax
import jax.numpy as jnp
from jax import lax
from jax.sharding import PartitionSpec as P

CHI = 8192
D = 4
PANEL = 512


def passed_along(block, axis, distance):
    devices = range(lax.axis_size(axis))
    route = [((i - distance) % len(devices), i) for i in devices]
    return lax.ppermute(block, axis, route)


def enlarge(raw_block, vertex_weights):
    row_count = raw_block.shape[0] // D
    split_block = raw_block.reshape(row_count, D, D, PANEL // D)
    mixed_block = jnp.einsum(
        "isub,sut->istb", split_block, vertex_weights, precision=lax.Precision.HIGHEST
    )
    return mixed_block.reshape(row_count * D, PANEL).astype(jnp.bfloat16)


def contract_rows(previous, hidden_panel):
    return jnp.dot(
        previous,
        lax.all_gather(hidden_panel, "bond", axis=0, tiled=True),
        preferred_element_type=jnp.float32,
    )


def build_hidden(corner_rows, panel_rows):
    first_sum = jnp.dot(
        corner_rows,
        lax.all_gather(panel_rows, "bond", axis=0, tiled=True),
        preferred_element_type=jnp.float32,
    )
    return (first_sum,)


def on_device(corner_mat, edge_mat, edge_panel, vertex_weights, projector, edge_projector):
    corner_rows = corner_mat[0]
    own_edge = edge_mat[0]
    panel_rows = edge_panel[0]
    proj_local = projector[0]
    edge_proj_local = edge_projector[0]
    sums = build_hidden(corner_rows, panel_rows)
    new_edge = lax.psum_scatter(
        jnp.dot(edge_proj_local.T, panel_rows, preferred_element_type=jnp.float32),
        "bond",
        scatter_dimension=0,
        tiled=True,
    ).astype(jnp.bfloat16)
    hidden_panel = sums[0].astype(jnp.bfloat16)
    previous = passed_along(own_edge, "dir", 1)
    enlarged = enlarge(contract_rows(previous, hidden_panel), vertex_weights)
    projected = jnp.dot(enlarged, proj_local, preferred_element_type=jnp.float32)
    new_corner = projected.astype(jnp.bfloat16)
    partial_full = jnp.dot(enlarged.T, enlarged, preferred_element_type=jnp.float32)
    gram_slab = lax.psum_scatter(partial_full, "bond", scatter_dimension=0, tiled=True)
    slab_rows = gram_slab.shape[0]
    proj_float = proj_local.astype(jnp.float32)
    right_side = jnp.dot(gram_slab, proj_float, precision=lax.Precision.HIGHEST)
    proj_slab = lax.dynamic_slice_in_dim(
        proj_float, lax.axis_index("bond") * slab_rows, slab_rows, 0
    )
    partial_keep = jnp.dot(proj_slab.T, right_side, precision=lax.Precision.HIGHEST)
    gram = lax.psum_scatter(partial_keep, "bond", scatter_dimension=0, tiled=True) / (CHI * D)
    return (new_corner[None], gram[None], new_edge[None])


def solution(mesh):
    in_specs = (
        P("dir", "bond", None),
        P("dir", "bond", None),
        P("dir", "bond", None),
        P(),
        P("dir", None, None),
        P("dir", "bond", None),
    )
    out_specs = (P("dir", "bond", None), P("dir", "bond", None), P("dir", "bond", None))
    return jax.shard_map(
        on_device, mesh=mesh, in_specs=in_specs, out_specs=out_specs, check_vma=False
    )
```

profile of v0, /device:TPU:0, one launch (start us, length us, event | category | flops | bytes accessed | tf_op | source)
XLA Modules:
  0.0 1017.8 jit_solution(17166629243554729927)
XLA Ops:
  7.2 0.5 collective-permute-start
  7.7 0.2 all-gather.6.cloned.1.call-update
  8.0 129.8 %all-gather.6.cloned.1.call-done = bf16[1,8192,512]{2,1,0:T(8,128)(2,1)} async-done(((bf16[1,1024,512]{2,1,0:T(8,128)(2,1)}), bf16[1,8192,512]{2,1,0:T(8,128)(2,1)}) %all-gather.6.cloned.1.call-update) | async-done | bytes 8388624 | tf_op jit(solution)/shard_map/all_gather | solution.py:37
  137.8 15.5 %fusion.17 = bf16[1024,512]{1,0:T(8,128)(2,1)} fusion(bf16[1,8192,512]{2,1,0:T(8,128)(2,1)} %all-gather.6.cloned.1.call-done, bf16[1,1024,8192]{2,1,0:T(8,128)(2,1)} %param.6), kind=kOutput, calls=%fused_computation.15 | convolution fusion | flops 8590458880 | bytes 26214400 | tf_op jit(solution)/shard_map/dot_general | solution.py:35
  153.4 0.2 reduce-scatter.4.cloned.1.call-start
  153.6 123.0 %all-gather.4.cloned.1.call-done = bf16[8192,512]{1,0:T(8,128)(2,1)} async-done(((bf16[1024,512]{1,0:T(8,128)(2,1)}), bf16[8192,512]{1,0:T(8,128)(2,1)}) %all-gather.4.cloned.1.call-update) | async-done | bytes 8388624 | tf_op jit(solution)/shard_map/all_gather | solution.py:29
  276.6 453.6 %collective-permute-done = bf16[4096,8192]{1,0:T(8,128)(2,1)} collective-permute-done((bf16[4096,8192]{1,0:T(8,128)(2,1)}, bf16[4096,8192]{1,0:T(8,128)(2,1)}, u32[]{:S(2)}, u32[]{:S(2)}) %collective-permute-start) | collective-permute-done | bytes 67108896 | tf_op jit(solution)/shard_map/ppermute | solution.py:14
  730.3 43.2 %convolution_bitcast_fusion = f32[4096,512]{0,1:T(8,128)} fusion(bf16[8192,512]{1,0:T(8,128)(2,1)} %all-gather.4.cloned.1.call-done, bf16[4096,8192]{1,0:T(8,128)(2,1)} %collective-permute-done), kind=kOutput, calls=%fused_computation.5 | convolution fusion | flops 34359738368 | bytes 83886080 | tf_op jit(solution)/shard_map/dot_general | solution.py:27
  773.5 9.0 copy.11
  782.5 9.9 reshape.14
  792.4 17.0 %fusion.12 = bf16[1024,4,4,128]{3,2,0,1:T(4,128)(2,1)S(1)} fusion(f32[1024,4,4,128]{3,2,1,0:T(4,128)} %reshape.14, f32[4,4,4]{2,1,0:T(4,128)S(1)} %copy-done.4), kind=kOutput, calls=%fused_computation.12 | convolution fusion | flops 102760448 | bytes 12583168 | tf_op jit(solution)/shard_map/isub,sut->istb/dot_general | solution.py:20
  809.4 1.4 copy.14
  810.9 1.9 copy-done.1
  812.8 3.3 fusion.9
  816.1 0.0 reduce-scatter.8.cloned.1.call-start
  816.2 1.3 fusion.22
  817.6 64.4 %reduce-scatter.4.cloned.1.call-done = f32[64,512]{1,0:T(8,128)} async-done(((f32[512,512]{1,0:T(8,128)}), f32[64,512]{1,0:T(8,128)}) %reduce-scatter.4.cloned.1.call-update) | async-done | bytes 131088 | tf_op jit(solution)/shard_map/reduce_scatter | solution.py:62
  881.9 1.2 fusion.25
  883.1 1.0 fusion.28
  884.1 62.3 %reduce-scatter.8.cloned.1.call-done = f32[32,512]{1,0:T(8,128)} async-done(((f32[256,512]{1,0:T(8,128)}), f32[32,512]{1,0:T(8,128)}) %reduce-scatter.8.cloned.1.call-update) | async-done | bytes 65552 | tf_op jit(solution)/shard_map/reduce_scatter | solution.py:50
  946.4 1.5 convert_bitcast_fusion
  947.9 4.8 fusion.5
  952.7 57.3 %reduce-scatter.6.cloned.1.call-done = f32[32,256]{1,0:T(8,128)} async-done(((f32[256,256]{1,0:T(8,128)}), f32[32,256]{1,0:T(8,128)}) %reduce-scatter.6.cloned.1.call-update) | async-done | bytes 32784 | tf_op jit(solution)/shard_map/reduce_scatter | solution.py:70
  1009.9 1.4 multiply_bitcast_fusion
  (16 shorter events, 0.2 us)
Async XLA Ops:
  7.2 809.0 %copy-start = (bf16[1,1024,256]{2,1,0:T(8,128)(2,1)S(1)}, bf16[1,1024,256]{2,1,0:T(8,128)(2,1)}, u32[]{:S(2)}) copy-start(bf16[1,1024,256]{2,1,0:T(8,128)(2,1)} %param.11) | copy-start | bytes 1572868
  7.2 130.6 %all-gather.6.cloned.1.call-start = ((), (), s32[]{:S(2)}) async-start(), calls=%async_computation.7 | async-start | bytes 9437184 | tf_op jit(solution)/shard_map/all_gather | solution.py:37
  7.2 723.1 %collective-permute-start = (bf16[4096,8192]{1,0:T(8,128)(2,1)}, bf16[4096,8192]{1,0:T(8,128)(2,1)}, u32[]{:S(2)}, u32[]{:S(2)}) collective-permute-start(bf16[4096,8192]{1,0:T(8,128)(2,1)} %bitcast.2), channel_id=1, source_target_pairs={{24,0},{0,8},{8,16},{16,24},{25,1},{1,9},{9,17},{17,25},{26,2},{2,... | collective-permute-start | bytes 201326592 | tf_op jit(solution)/shard_map/ppermute | solution.py:14
  7.9 268.7 %all-gather.4.cloned.1.call-start = ((), (), s32[]{:S(2)}) async-start(), calls=%async_computation.3 | async-start | bytes 9437184 | tf_op jit(solution)/shard_map/all_gather | solution.py:29
  153.4 728.5 %reduce-scatter.4.cloned.1.call-start = ((), (), s32[]{:S(2)}) async-start(), calls=%async_computation.4 | async-start | bytes 1179648 | tf_op jit(solution)/shard_map/reduce_scatter | solution.py:62
  782.5 9.9 copy-start.4
  810.8 2.0 copy-start.1
  810.9 5.4 copy-start.2
  812.8 69.1 %copy-start.3 = (bf16[1,512,256]{2,1,0:T(8,128)(2,1)S(1)}, bf16[1,512,256]{2,1,0:T(8,128)(2,1)}, u32[]{:S(2)}) copy-start(bf16[1,512,256]{2,1,0:T(8,128)(2,1)} %param.10) | copy-start | bytes 786436
  816.1 130.3 %reduce-scatter.8.cloned.1.call-start = ((), (), s32[]{:S(2)}) async-start(), calls=%async_computation.6 | async-start | bytes 589824 | tf_op jit(solution)/shard_map/reduce_scatter | solution.py:50
  817.5 192.4 %reduce-scatter.6.cloned.1.call-start = ((), (), s32[]{:S(2)}) async-start(), calls=%async_computation.5 | async-start | bytes 294912 | tf_op jit(solution)/shard_map/reduce_scatter | solution.py:70
Sparse Core Ops, SparseCore 0:
  10.1 127.6 all-gather.5
  153.5 123.1 all-gather.3
  816.3 65.5 reduce-scatter.3
  885.5 60.9 reduce-scatter.7
  949.6 60.2 reduce-scatter.5
where the time goes:
time: 1020 us
  waiting for transfers between devices  891 us (87%)
  matrix products  87.2 us (9%)
  local copies, waits for them, and re-layouts  22.3 us (2%)
  between operations  13.8 us (1%)
    ppermute x1, waiting for transfers between devices, passed_along(): return lax.ppermute(block, axis, route)  454 us
    all_gather x1, waiting for transfers between devices, build_hidden(): lax.all_gather(panel_rows, 'bond', axis=0, tiled=True)  130 us
    all_gather x1, waiting for transfers between devices, contract_rows(): lax.all_gather(hidden_panel, 'bond', axis=0, tiled=True)  123 us
    reduce_scatter x1, waiting for transfers between devices, on_device(): lax.psum_scatter(partial_full, 'bond', scatter_dimension=0, tiled=True)  64.4 us
    reduce_scatter x1, waiting for transfers between devices, on_device(): lax.psum_scatter(jnp.dot(edge_proj_local.T, panel_rows, preferred_element...  62.3 us
    reduce_scatter x1, waiting for transfers between devices, on_device(): lax.psum_scatter(partial_keep, 'bond', scatter_dimension=0, tiled=True)  57.3 us
    dot_general x1, matrix products, contract_rows(): jnp.dot(previous, lax.all_gather(hidden_panel, 'bond', axis=0, tiled=True...  43.2 us
  transfers between devices with their start and end apart: 6, of which 6 were waited for; matrix products, arithmetic and copies ran while one was open for 2% of the time, Pallas kernels for 0%

commit v1 on v0

v1 whole, which is shorter than its diff:
```python
import jax
import jax.numpy as jnp
from jax import lax
from jax.sharding import PartitionSpec as P

D = 4


def to_lower(block):
    n = lax.axis_size("dir")
    return lax.ppermute(block, "dir", [(i, (i - 1) % n) for i in range(n)])


def to_upper(block):
    n = lax.axis_size("dir")
    return lax.ppermute(block, "dir", [(i, (i + 1) % n) for i in range(n)])


def on_device(corner_mat, edge_mat, edge_panel, vertex_weights, projector, edge_projector):
    corner_rows = corner_mat[0]
    own_edge = edge_mat[0]
    panel_rows = edge_panel[0]
    n_dir = lax.axis_size("dir")
    rows, panel = own_edge.shape[0], panel_rows.shape[1]
    chi = own_edge.shape[1]
    gathered = lax.all_gather(panel_rows, "bond", axis=0, tiled=True)
    hidden = jnp.dot(corner_rows, gathered, preferred_element_type=jnp.float32).astype(jnp.bfloat16)
    new_edge = lax.psum_scatter(
        jnp.dot(edge_projector[0].T, panel_rows, preferred_element_type=jnp.float32),
        "bond", scatter_dimension=0, tiled=True,
    ).astype(jnp.bfloat16)
    upper_hidden = lax.all_gather(to_lower(hidden), "bond", axis=0, tiled=True)
    upper_proj = to_lower(projector[0])
    raw = jnp.dot(own_edge, upper_hidden, preferred_element_type=jnp.float32)
    coef = jnp.tile(vertex_weights, (rows // D, 1, 1))
    parts = [raw[:, u * (panel // D):(u + 1) * (panel // D)] for u in range(D)]
    mixed = [
        sum(coef[:, u, t][:, None] * parts[u] for u in range(D)) for t in range(D)
    ]
    enlarged = jnp.concatenate(mixed, axis=1).astype(jnp.bfloat16)
    projected = jnp.dot(enlarged, upper_proj, preferred_element_type=jnp.float32)
    new_corner = to_upper(projected.astype(jnp.bfloat16))
    high = projected.astype(jnp.bfloat16)
    low = (projected - high.astype(jnp.float32)).astype(jnp.bfloat16)
    cross = jnp.dot(high.T, low, preferred_element_type=jnp.float32)
    partial = jnp.dot(high.T, high, preferred_element_type=jnp.float32) + cross + cross.T
    gram = to_upper(lax.psum_scatter(partial, "bond", scatter_dimension=0, tiled=True)) / (chi * D)
    return (new_corner[None], gram[None], new_edge[None])


def solution(mesh):
    in_specs = (
        P("dir", "bond", None),
        P("dir", "bond", None),
        P("dir", "bond", None),
        P(),
        P("dir", None, None),
        P("dir", "bond", None),
    )
    out_specs = (P("dir", "bond", None), P("dir", "bond", None), P("dir", "bond", None))
    return jax.shard_map(
        on_device, mesh=mesh, in_specs=in_specs, out_specs=out_specs, check_vma=False
    )
```

time: 1020 us -> 481 us (0.47)
  waiting for transfers between devices: 891 us -> 375 us
  matrix products: 87.2 us -> 66.5 us
    ppermute x1 -> x4, waiting for transfers between devices: 454 us -> 12.3 us  [the longest x2 12.3 us: to_lower(): return lax.ppermute(block, 'dir', [(i, (i - 1) % n) for i in range(n)])]
    reduce_scatter x3 -> x2, waiting for transfers between devices: 184 us -> 123 us  [the longest x1 64.2 us: on_device(): lax.psum_scatter(jnp.dot(edge_projector[0].T, panel_rows, preferred_eleme...]
    dot_general x8 -> x6, matrix products: 87.2 us -> 66.5 us  [the longest x1 42.2 us: on_device(): raw = jnp.dot(own_edge, upper_hidden, preferred_element_type=jnp.float32)]
    all_gather x2, waiting for transfers between devices: 253 us -> 239 us  [the longest x1 130 us: on_device(): gathered = lax.all_gather(panel_rows, 'bond', axis=0, tiled=True)]
    another operation x0 -> x2, local copies, waits for them, and re-layouts: none -> 12.4 us  [on_device(): coef = jnp.tile(vertex_weights, (rows // D, 1, 1))]
  transfers between devices with their start and end apart: 6 -> 8, of which waited for: 6 -> 5; matrix products, arithmetic and copies ran while one was open for 2% -> 14% of each run, Pallas kernels for 0% -> 0%
where the time goes in v1:
time: 481 us
  waiting for transfers between devices  375 us (78%)
  matrix products  66.5 us (14%)
  local copies, waits for them, and re-layouts  18.8 us (4%)
  between operations  13.9 us (3%)
    all_gather x1, waiting for transfers between devices, on_device(): gathered = lax.all_gather(panel_rows, 'bond', axis=0, tiled=True)  130 us
    all_gather x1, waiting for transfers between devices, on_device(): upper_hidden = lax.all_gather(to_lower(hidden), 'bond', axis=0, tiled=True)  109 us
    reduce_scatter x1, waiting for transfers between devices, on_device(): lax.psum_scatter(jnp.dot(edge_projector[0].T, panel_rows, preferred_eleme...  64.2 us
    reduce_scatter x1, waiting for transfers between devices, on_device(): lax.psum_scatter(partial, 'bond', scatter_dimension=0, tiled=True)  58.4 us
    dot_general x1, matrix products, on_device(): raw = jnp.dot(own_edge, upper_hidden, preferred_element_type=jnp.float32)  42.2 us
    dot_general x1, matrix products, on_device(): jnp.dot(corner_rows, gathered, preferred_element_type=jnp.float32)  14.8 us
    another operation x2, local copies, waits for them, and re-layouts, on_device(): coef = jnp.tile(vertex_weights, (rows // D, 1, 1))  12.4 us
    ppermute x2, waiting for transfers between devices, to_lower(): return lax.ppermute(block, 'dir', [(i, (i - 1) % n) for i in range(n)])  12.3 us
  transfers between devices with their start and end apart: 8, of which 5 were waited for; matrix products, arithmetic and copies ran while one was open for 14% of the time, Pallas kernels for 0%

profile of v1, /device:TPU:0, one launch (start us, length us, event | category | flops | bytes accessed | tf_op | source)
XLA Modules:
  0.0 481.2 jit_solution(3838824658602017020)
XLA Ops:
  7.2 0.7 all-gather.6.cloned.1.call-update
  8.0 129.8 %all-gather.6.cloned.1.call-done = bf16[1,8192,512]{2,1,0:T(8,128)(2,1)} async-done(((bf16[1,1024,512]{2,1,0:T(8,128)(2,1)}), bf16[1,8192,512]{2,1,0:T(8,128)(2,1)}) %all-gather.6.cloned.1.call-update) | async-done | bytes 8388624 | tf_op jit(solution)/shard_map/all_gather | solution.py:26
  137.8 14.8 %fusion.17 = bf16[1024,512]{1,0:T(8,128)(2,1)S(1)} fusion(bf16[1,8192,512]{2,1,0:T(8,128)(2,1)} %all-gather.6.cloned.1.call-done, bf16[1,1024,8192]{2,1,0:T(8,128)(2,1)} %param.6), kind=kOutput, calls=%fused_computation.20 | convolution fusion | flops 8590458880 | bytes 26214400 | tf_op jit(solution)/shard_map/dot_general | solution.py:27
  152.6 0.6 collective-permute-start
  153.1 12.3 %collective-permute-done = bf16[1024,512]{1,0:T(8,128)(2,1)S(1)} collective-permute-done((bf16[1024,512]{1,0:T(8,128)(2,1)S(1)}, bf16[1024,512]{1,0:T(8,128)(2,1)S(1)}, u32[]{:S(2)}, u32[]{:S(2)}) %collective-permute-start) | collective-permute-done | bytes 1048608 | tf_op jit(solution)/shard_map/ppermute | solution.py:11
  165.4 1.0 copy-done.3
  166.5 2.1 collective-permute-start.1
  168.8 3.8 tile.4
  172.5 8.6 %tile.10 = f32[4096,4,4]{0,2,1:T(4,128)S(1)} reshape(f32[1024,4,4,4]{1,0,3,2:T(8,128)} %tile.4) | data formatting | bytes 524288 | tf_op jit(solution)/shard_map/tile | solution.py:35
  181.1 0.2 fusion.29
  181.3 109.3 %all-gather.4.cloned.1.call-done = bf16[8192,512]{1,0:T(8,128)(2,1)} async-done(((bf16[1024,512]{1,0:T(8,128)(2,1)}), bf16[8192,512]{1,0:T(8,128)(2,1)}) %all-gather.4.cloned.1.call-update) | async-done | bytes 8388624 | tf_op jit(solution)/shard_map/all_gather | solution.py:32
  290.7 42.2 %fusion.5 = f32[4096,512]{0,1:T(8,128)S(1)} fusion(bf16[8192,512]{1,0:T(8,128)(2,1)} %all-gather.4.cloned.1.call-done, bf16[1,4096,8192]{2,1,0:T(8,128)(2,1)} %param.7), kind=kOutput, calls=%fused_computation.5 | convolution fusion | flops 34359738368 | bytes 83886080 | tf_op jit(solution)/shard_map/dot_general | solution.py:34
  332.9 1.1 add_convert_fusion.3
  334.0 1.1 add_convert_fusion.1
  335.1 2.5 fusion.30
  337.6 1.9 copy-done.1
  339.5 0.8 fusion.16
  340.5 5.0 %fusion.22 = f32[256,256]{1,0:T(8,128)} fusion(f32[256,256]{1,0:T(8,128)S(1)} %fusion.16, f32[256,256]{0,1:T(8,128)S(1)} %copy.13, f32[4096,256]{1,0:T(8,128)} %copy-done.1), kind=kOutput, calls=%fused_computation.22 | convolution fusion | flops 538050560 | bytes 4980736 | tf_op jit(solution)/shard_map/dot_general | solution.py:46
  345.6 1.2 fusion.23
  346.9 58.4 %reduce-scatter.3.cloned.1.call-done = f32[32,256]{1,0:T(8,128)} async-done(((f32[256,256]{1,0:T(8,128)}), f32[32,256]{1,0:T(8,128)}) %reduce-scatter.3.cloned.1.call-update) | async-done | bytes 32784 | tf_op jit(solution)/shard_map/reduce_scatter | solution.py:47
  405.3 64.2 %reduce-scatter.5.cloned.1.call-done = f32[32,512]{1,0:T(8,128)} async-done(((f32[256,512]{1,0:T(8,128)}), f32[32,512]{1,0:T(8,128)}) %reduce-scatter.5.cloned.1.call-update) | async-done | bytes 65552 | tf_op jit(solution)/shard_map/reduce_scatter | solution.py:28
  469.6 1.5 convert_bitcast_fusion
  471.0 0.6 multiply_bitcast_fusion
  471.6 3.0 copy.15
  (24 shorter events, 0.5 us)
Async XLA Ops:
  7.2 338.4 %copy-start = (bf16[1,1024,256]{2,1,0:T(8,128)(2,1)S(1)}, bf16[1,1024,256]{2,1,0:T(8,128)(2,1)}, u32[]{:S(2)}) copy-start(bf16[1,1024,256]{2,1,0:T(8,128)(2,1)} %param.11) | copy-start | bytes 1572868
  7.2 130.6 %all-gather.6.cloned.1.call-start = ((), (), s32[]{:S(2)}) async-start(), calls=%async_computation.5 | async-start | bytes 9437184 | tf_op jit(solution)/shard_map/all_gather | solution.py:26
  7.9 158.6 %copy-start.5 = (bf16[1,512,256]{2,1,0:T(8,128)(2,1)S(1)}, bf16[1,512,256]{2,1,0:T(8,128)(2,1)}, u32[]{:S(2)}) copy-start(bf16[1,512,256]{2,1,0:T(8,128)(2,1)} %param.10) | copy-start | bytes 786436
  7.9 160.7 %copy-start.4 = (f32[4,4,4]{2,1,0:T(4,128)S(1)}, f32[4,4,4]{2,1,0:T(4,128)}, u32[]{:S(2)}) copy-start(f32[4,4,4]{2,1,0:T(4,128)} %param.9) | copy-start | bytes 772
  7.9 282.8 %all-gather.4.cloned.1.call-start = ((), (), s32[]{:S(2)}) async-start(), calls=%async_computation.2 | async-start | bytes 9437184 | tf_op jit(solution)/shard_map/all_gather | solution.py:32
  152.6 12.9 %collective-permute-start = (bf16[1024,512]{1,0:T(8,128)(2,1)S(1)}, bf16[1024,512]{1,0:T(8,128)(2,1)S(1)}, u32[]{:S(2)}, u32[]{:S(2)}) collective-permute-start(bf16[1024,512]{1,0:T(8,128)(2,1)S(1)} %fusion.17), channel_id=1, source_target_pairs={{0,24},{8,0},{16,8},{24,16},{1,25},{9,1},{17,9},{25,17},{2,26},{10... | collective-permute-start | bytes 3145736 | tf_op jit(solution)/shard_map/ppermute | solution.py:11
  165.4 1.0 copy-start.3
  166.4 238.9 %reduce-scatter.3.cloned.1.call-start = ((), (), s32[]{:S(2)}) async-start(), calls=%async_computation.3 | async-start | bytes 294912 | tf_op jit(solution)/shard_map/reduce_scatter | solution.py:47
  166.5 168.6 %collective-permute-start.1 = (bf16[512,256]{1,0:T(8,128)(2,1)S(1)}, bf16[512,256]{1,0:T(8,128)(2,1)S(1)}, u32[]{:S(2)}, u32[]{:S(2)}) collective-permute-start(bf16[512,256]{1,0:T(8,128)(2,1)S(1)} %bitcast.69), channel_id=1, source_target_pairs={{0,24},{8,0},{16,8},{24,16},{1,25},{9,1},{17,9},{25,17},{2,26},{10... | collective-permute-start | bytes 786440 | tf_op jit(solution)/shard_map/ppermute | solution.py:11
  337.6 1.9 copy-start.1
  340.4 5.2 %copy-start.2 = (bf16[1,1024,512]{2,1,0:T(8,128)(2,1)S(1)}, bf16[1,1024,512]{2,1,0:T(8,128)(2,1)}, u32[]{:S(2)}) copy-start(bf16[1,1024,512]{2,1,0:T(8,128)(2,1)} %param.8) | copy-start | bytes 3145732
  340.4 131.2 %collective-permute-start.2 = (bf16[4096,256]{1,0:T(8,128)(2,1)}, bf16[4096,256]{1,0:T(8,128)(2,1)}, u32[]{:S(2)}, u32[]{:S(2)}) collective-permute-start(bf16[4096,256]{1,0:T(8,128)(2,1)} %get-tuple-element.23), channel_id=1, source_target_pairs={{0,8},{8,16},{16,24},{24,0},{1,9},{9,17},{17,25},{25,1},{2,10},{10... | collective-permute-start | bytes 6291464 | tf_op jit(solution)/shard_map/ppermute | solution.py:16
  345.5 124.0 %reduce-scatter.5.cloned.1.call-start = ((), (), s32[]{:S(2)}) async-start(), calls=%async_computation.4 | async-start | bytes 589824 | tf_op jit(solution)/shard_map/reduce_scatter | solution.py:28
  405.3 65.7 %collective-permute-start.3 = (f32[32,256]{1,0:T(8,128)}, f32[32,256]{1,0:T(8,128)S(1)}, u32[]{:S(2)}, u32[]{:S(2)}) collective-permute-start(f32[32,256]{1,0:T(8,128)} %reduce-scatter.3.cloned.1.call-done), channel_id=1, source_target_pairs={{0,8},{8,16},{16,24},{24,0},{1,9},{9,17},{17,25},{25,1},{2,10},{10... | collective-permute-start | bytes 98312 | tf_op jit(solution)/shard_map/ppermute | solution.py:16
Sparse Core Ops, SparseCore 0:
  10.1 127.6 all-gather.5
  166.6 124.0 all-gather.3
  345.6 59.6 reduce-scatter.2
  408.5 61.0 reduce-scatter.4

commit v2 on v1

--- a/solution.py
+++ b/solution.py
@@ -1,9 +1,340 @@
+import functools
+
 import jax
 import jax.numpy as jnp
 from jax import lax
+from jax.experimental import pallas as pl
+from jax.experimental.pallas import tpu as pltpu
 from jax.sharding import PartitionSpec as P
 
 D = 4
+PIECES = 2
+DEPTH = 3
+TILE = 512
+MESH = pl.DeviceIdType.MESH
+F32 = jnp.float32
+BF16 = jnp.bfloat16
+
+
+def over_rows(left, right):
+    return lax.dot_general(left, right, (((0,), (0,)), ((), ())), preferred_element_type=F32)
+
+
+def fused_kernel(
+    n, n_dir,
+    c_ref, a_ref, e_ref, f_ref, p_ref, w_ref,
+    corner_out, gram_out, edge_out,
+    e_all, h_all, raw_sum, hid_sum, hid, a_buf, c_buf, out_buf, p_up,
+    edge_part, edge_recv, gram_high, gram_cross, gram_part, gram_recv,
+    e_send, e_recv, h_send, h_recv, c_sem, a_sem, hid_send, hid_recv,
+    p_send, p_recv, out_send, out_recv, es_send, es_recv, g_send, g_recv, go,
+):
+    k = lax.axis_index("dir")
+    b = lax.axis_index("bond")
+    up, down = lax.rem(k + 1, n_dir), lax.rem(k + n_dir - 1, n_dir)
+    odd_dir = lax.rem(k, 2)
+    odd = lax.rem(b, 2)
+    pos = (1 - odd) * (b // 2) + odd * (n - 1 - b // 2)
+
+    def bond_at(place):
+        place = lax.rem(place, n)
+        back = place // (n // 2)
+        return (1 - back) * (2 * place) + back * (2 * (n - 1 - place) + 1)
+
+    right, left = bond_at(pos + 1), bond_at(pos + n - 1)
+    rows = e_ref.shape[0]
+    half = rows // 2
+    piece = half // PIECES
+    total_rows = a_ref.shape[0]
+    chunks = 2 * n
+
+    barrier = pltpu.get_barrier_semaphore()
+    for j in range(n):
+        if j > 0:
+            pl.semaphore_signal(barrier, inc=1, device_id=(k, lax.rem(b + j, n)), device_id_type=MESH)
+        pl.semaphore_signal(barrier, inc=1, device_id=(up, lax.rem(b + j, n)), device_id_type=MESH)
+        pl.semaphore_signal(barrier, inc=1, device_id=(down, lax.rem(b + j, n)), device_id_type=MESH)
+
+    def columns(j):
+        way, hops = lax.rem(j, 2), j // 2
+        owner = bond_at(pos + (1 - way) * (n - hops) + way * hops)
+        return pl.ds(pl.multiple_of(owner * rows + way * half, half), half)
+
+    def c_load(j):
+        return pltpu.make_async_copy(c_ref.at[:, columns(j)], c_buf.at[lax.rem(j, DEPTH)], c_sem.at[lax.rem(j, DEPTH)])
+
+    def a_load(j):
+        return pltpu.make_async_copy(a_ref.at[:, columns(j)], a_buf.at[lax.rem(j, DEPTH)], a_sem.at[lax.rem(j, DEPTH)])
+
+    for j in range(DEPTH - 1):
+        c_load(j).start()
+        a_load(j).start()
+
+    e_all[0, 0] = e_ref[:half]
+    e_all[1, 0] = e_ref[half:]
+
+    def hop(panels, sends, recvs, way, slot, q):
+        part = pl.ds(q * piece, piece)
+        return pltpu.make_async_remote_copy(
+            src_ref=panels.at[way, slot, part],
+            dst_ref=panels.at[way, slot + 1, part],
+            send_sem=sends.at[way, slot, q],
+            recv_sem=recvs.at[way, slot, q],
+            device_id=(k, left if way else right),
+            device_id_type=MESH,
+        )
+
+    def start_ring(panels, sends, recvs):
+        for q in range(PIECES):
+            for way in range(2):
+                hop(panels, sends, recvs, way, 0, q).start()
+
+    def run_ring(panels, sends, recvs, add, gate):
+        add(0, True)
+
+        @pl.loop(1, n)
+        def _(s):
+            for q in range(PIECES):
+                for way in range(2):
+                    hop(panels, sends, recvs, way, s - 1, q).wait_recv()
+
+                    @pl.when(s < n - 1)
+                    def _():
+                        hop(panels, sends, recvs, way, s, q).start()
+
+                if q == PIECES - 1:
+                    @pl.when(s == n - 2)
+                    def _():
+                        gate()
+                add(2 * s - 1 + q, False)
+
+    def end_ring(panels, sends, recvs):
+        @pl.loop(0, n - 1)
+        def _(s):
+            for q in range(PIECES):
+                for way in range(2):
+                    hop(panels, sends, recvs, way, s, q).wait_send()
+
+    def prefetch(load, j):
+        @pl.when(j + DEPTH - 1 < chunks)
+        def _():
+            load(j + DEPTH - 1).start()
+
+    def add_hidden(j, first):
+        prefetch(c_load, j)
+        c_load(j).wait()
+        slot = lax.rem(j, DEPTH)
+        way, hops = lax.rem(j, 2), j // 2
+
+        @pl.loop(0, rows // TILE)
+        def _(r):
+            span = pl.ds(pl.multiple_of(r * TILE, TILE), TILE)
+            term = jnp.dot(c_buf[slot, span, :], e_all[way, hops], preferred_element_type=F32)
+            hid_sum[span, :] = term if first else hid_sum[span, :] + term
+
+    def add_raw(j, first):
+        prefetch(a_load, j)
+        a_load(j).wait()
+        slot = lax.rem(j, DEPTH)
+        way, hops = lax.rem(j, 2), j // 2
+
+        @pl.loop(0, total_rows // TILE)
+        def _(r):
+            span = pl.ds(pl.multiple_of(r * TILE, TILE), TILE)
+            term = jnp.dot(a_buf[slot, span, :], h_all[way, hops], preferred_element_type=F32)
+            raw_sum[span, :] = term if first else raw_sum[span, :] + term
+
+    pl.semaphore_wait(barrier, 3 * n - 1)
+
+    p_copy = pltpu.make_async_remote_copy(
+        src_ref=p_ref, dst_ref=p_up, send_sem=p_send, recv_sem=p_recv,
+        device_id=(down, b), device_id_type=MESH,
+    )
+
+    def edge_copy(j):
+        target = lax.rem(b + j, n)
+        return pltpu.make_async_remote_copy(
+            src_ref=edge_part.at[target], dst_ref=edge_recv.at[j],
+            send_sem=es_send.at[j], recv_sem=es_recv.at[j],
+            device_id=(k, target), device_id_type=MESH,
+        )
+
+    @pl.when(odd_dir == 1)
+    def _():
+        pl.semaphore_wait(go, 1)
+
+    start_ring(e_all, e_send, e_recv)
+    p_copy.start()
+
+    slab = edge_part.shape[1]
+    keep = f_ref.shape[1]
+    edge_sum = over_rows(f_ref[...], e_ref[...])
+    for r in range(n):
+        edge_part[r] = edge_sum[r * slab:(r + 1) * slab]
+    for j in range(1, n):
+        edge_copy(j).start()
+
+    def open_odd():
+        @pl.when(odd_dir == 0)
+        def _():
+            pl.semaphore_signal(go, inc=1, device_id=(up, b), device_id_type=MESH)
+
+    def open_even():
+        @pl.when(odd_dir == 1)
+        def _():
+            pl.semaphore_signal(go, inc=1, device_id=(down, b), device_id_type=MESH)
+
+    run_ring(e_all, e_send, e_recv, add_hidden, open_odd)
+    add_hidden(chunks - 1, False)
+    hid[...] = hid_sum[...].astype(BF16)
+
+    def hid_copy(way):
+        return pltpu.make_async_remote_copy(
+            src_ref=hid.at[pl.ds(way * half, half)], dst_ref=h_all.at[way, 0],
+            send_sem=hid_send.at[way], recv_sem=hid_recv.at[way],
+            device_id=(down, b), device_id_type=MESH,
+        )
+
+    for way in range(2):
+        hid_copy(way).start()
+    end_ring(e_all, e_send, e_recv)
+
+    for j in range(1, n):
+        edge_copy(j).wait()
+    edge_total = edge_part[b]
+    for j in range(1, n):
+        edge_total = edge_total + edge_recv[j]
+    edge_out[...] = edge_total.astype(BF16)
+
+    for way in range(2):
+        hid_copy(way).wait()
+
+    @pl.when(odd_dir == 0)
+    def _():
+        pl.semaphore_wait(go, 1)
+
+    start_ring(h_all, h_send, h_recv)
+    run_ring(h_all, h_send, h_recv, add_raw, open_even)
+
+    p_copy.wait()
+    last = chunks - 1
+    a_load(last).wait()
+    gram_high[...] = jnp.zeros_like(gram_high)
+    gram_cross[...] = jnp.zeros_like(gram_cross)
+    width = e_ref.shape[1] // D
+
+    def out_copy(r):
+        span = pl.ds(pl.multiple_of(r * TILE, TILE), TILE)
+        return pltpu.make_async_remote_copy(
+            src_ref=out_buf.at[span], dst_ref=corner_out.at[span],
+            send_sem=out_send.at[r], recv_sem=out_recv.at[r],
+            device_id=(up, b), device_id_type=MESH,
+        )
+
+    @pl.loop(0, total_rows // TILE)
+    def _(r):
+        span = pl.ds(pl.multiple_of(r * TILE, TILE), TILE)
+        raw = raw_sum[span, :] + jnp.dot(
+            a_buf[last % DEPTH, span, :], h_all[1, n - 1], preferred_element_type=F32
+        )
+        parts = [raw[:, u * width:(u + 1) * width].reshape(TILE // 8, 8, width) for u in range(D)]
+        mixed = []
+        for t in range(D):
+            total = parts[0] * w_ref[t][None]
+            for u in range(1, D):
+                total = total + parts[u] * w_ref[u * D + t][None]
+            mixed.append(total.reshape(TILE, width).astype(BF16))
+        projected = jnp.dot(jnp.concatenate(mixed, axis=1), p_up[...], preferred_element_type=F32)
+        high = projected.astype(BF16)
+        out_buf[span, :] = high
+        out_copy(r).start()
+        low = (projected - high.astype(F32)).astype(BF16)
+        gram_high[...] += over_rows(high, high)
+        gram_cross[...] += over_rows(high, low)
+
+    gram_sum = gram_high[...] + (gram_cross[...] + gram_cross[...].T)
+    g_slab = gram_part.shape[1]
+    for r in range(n):
+        gram_part[r] = gram_sum[r * g_slab:(r + 1) * g_slab]
+
+    def gram_copy(j):
+        target = lax.rem(b + j, n)
+        return pltpu.make_async_remote_copy(
+            src_ref=gram_part.at[target], dst_ref=gram_recv.at[j],
+            send_sem=g_send.at[j], recv_sem=g_recv.at[j],
+            device_id=(up, target), device_id_type=MESH,
+        )
+
+    for j in range(n):
+        gram_copy(j).start()
+    end_ring(h_all, h_send, h_recv)
+    for j in range(n):
+        gram_copy(j).wait()
+    gram_total = gram_recv[0]
+    for j in range(1, n):
+        gram_total = gram_total + gram_recv[j]
+    gram_out[...] = gram_total / (c_ref.shape[1] * D)
+
+    @pl.loop(0, total_rows // TILE)
+    def _(r):
+        out_copy(r).wait()
+
+
+def in_one_kernel(n, n_dir, corner_mat, edge_mat, edge_panel, vertex_weights, projector, edge_projector):
+    rows, panel = edge_panel.shape[1:]
+    total_rows = edge_mat.shape[1]
+    keep = projector.shape[2]
+    width = panel // D
+    half = rows // 2
+    piece_shape = (2, n - 1, PIECES)
+    tiles = total_rows // TILE
+    coef = jnp.broadcast_to(
+        jnp.tile(vertex_weights.transpose(1, 2, 0).reshape(D * D, D), (1, 8 // D))[:, :, None], (D * D, 8, width)
+    )
+    vmem = pl.BlockSpec(memory_space=pltpu.VMEM)
+    anywhere = pl.BlockSpec(memory_space=pl.ANY)
+    dma = pltpu.SemaphoreType.DMA
+    flops = 2 * panel * corner_mat.shape[2] * (rows + total_rows)
+    corner, gram, edge = pl.pallas_call(
+        functools.partial(fused_kernel, n, n_dir),
+        out_shape=(
+            jax.ShapeDtypeStruct((total_rows, keep), BF16),
+            jax.ShapeDtypeStruct((keep // n, keep), F32),
+            jax.ShapeDtypeStruct((keep // n, panel), BF16),
+        ),
+        in_specs=[anywhere, anywhere, vmem, vmem, vmem, vmem],
+        out_specs=(anywhere, vmem, vmem),
+        scratch_shapes=[
+            pltpu.VMEM((2, n, half, panel), BF16),
+            pltpu.VMEM((2, n, half, panel), BF16),
+            pltpu.VMEM((total_rows, panel), F32),
+            pltpu.VMEM((rows, panel), F32),
+            pltpu.VMEM((rows, panel), BF16),
+            pltpu.VMEM((DEPTH, total_rows, half), BF16),
+            pltpu.VMEM((DEPTH, rows, half), BF16),
+            pltpu.VMEM((total_rows, keep), BF16),
+            pltpu.VMEM((panel, keep), BF16),
+            pltpu.VMEM((n, keep // n, panel), F32),
+            pltpu.VMEM((n, keep // n, panel), F32),
+            pltpu.VMEM((keep, keep), F32),
+            pltpu.VMEM((keep, keep), F32),
+            pltpu.VMEM((n, keep // n, keep), F32),
+            pltpu.VMEM((n, keep // n, keep), F32),
+            dma(piece_shape), dma(piece_shape), dma(piece_shape), dma(piece_shape),
+            dma((DEPTH,)), dma((DEPTH,)), dma((2,)), dma((2,)),
+            dma, dma, dma((tiles,)), dma((tiles,)),
+            dma((n,)), dma((n,)), dma((n,)), dma((n,)),
+            pltpu.SemaphoreType.REGULAR,
+        ],
+        compiler_params=pltpu.CompilerParams(
+            collective_id=0, has_side_effects=True, vmem_limit_bytes=60 * 1024 * 1024
+        ),
+        cost_estimate=pl.CostEstimate(
+            flops=flops, bytes_accessed=2 * corner_mat.shape[2] * (rows + total_rows), transcendentals=0
+        ),
+        name="corner_window",
+    )(corner_mat[0], edge_mat[0], edge_panel[0], edge_projector[0], projector[0], coef)
+    return (corner[None], gram[None], edge[None])
 
 
 def to_lower(block):
@@ -16,7 +347,7 @@
     return lax.ppermute(block, "dir", [(i, (i + 1) % n) for i in range(n)])
 
 
-def on_device(corner_mat, edge_mat, edge_panel, vertex_weights, projector, edge_projector):
+def in_many_ops(corner_mat, edge_mat, edge_panel, vertex_weights, projector, edge_projector):
     corner_rows = corner_mat[0]
     own_edge = edge_mat[0]
     panel_rows = edge_panel[0]
@@ -49,6 +380,9 @@
 
 
 def solution(mesh):
+    n, n_dir = mesh.shape["bond"], mesh.shape["dir"]
+    small = n % 2 == 0 and n_dir % 2 == 0 and n_dir > 2 and n <= 8
+    on_device = functools.partial(in_one_kernel, n, n_dir) if small else in_many_ops
     in_specs = (
         P("dir", "bond", None),
         P("dir", "bond", None),

time: 481 us -> 229 us (0.48)
  waiting for transfers between devices: 375 us -> 0 us
  Pallas kernels: 0 us -> 220 us
  matrix products: 66.5 us -> 0 us
  between operations: 13.9 us -> 0.64 us
  local copies, waits for them, and re-layouts: 18.8 us -> 7.37 us
    all_gather x2 -> x0, waiting for transfers between devices: 239 us -> none  [the longest x1 130 us: on_device(): gathered = lax.all_gather(panel_rows, 'bond', axis=0, tiled=True)]
    pallas_call x0 -> x1, Pallas kernels: none -> 220 us  [in_one_kernel(): pl.pallas_call(functools.partial(fused_kernel, n, n_dir), out_shape=(jax....]
    reduce_scatter x2 -> x0, waiting for transfers between devices: 123 us -> none  [the longest x1 64.2 us: on_device(): lax.psum_scatter(jnp.dot(edge_projector[0].T, panel_rows, preferred_eleme...]
    dot_general x6 -> x0, matrix products: 66.5 us -> none  [the longest x1 42.2 us: on_device(): raw = jnp.dot(own_edge, upper_hidden, preferred_element_type=jnp.float32)]
    ppermute x4 -> x0, waiting for transfers between devices: 12.3 us -> none  [the longest x2 12.3 us: to_lower(): return lax.ppermute(block, 'dir', [(i, (i - 1) % n) for i in range(n)])]
    another operation x2 -> x3, local copies, waits for them, and re-layouts: 12.4 us -> 0.86 us  [in_one_kernel(): jnp.tile(vertex_weights.transpose(1, 2, 0).reshape(D * D, D), (1, 8 // D))]
  transfers between devices with their start and end apart: 8 -> 0, of which waited for: 5 -> 0; matrix products, arithmetic and copies ran while one was open for 14% -> 0% of each run, Pallas kernels for 0% -> 0%
where the time goes in v2:
time: 229 us; the launch traced here: 228 us
  Pallas kernels  220 us (96%)
  local copies, waits for them, and re-layouts  7.37 us (3%)
    pallas_call x1, Pallas kernels, in_one_kernel(): pl.pallas_call(functools.partial(fused_kernel, n, n_dir), out_shape=(jax....  220 us
    unnamed x3, local copies, waits for them, and re-layouts  5.79 us

profile of v2, /device:TPU:0, one launch (start us, length us, event | category | flops | bytes accessed | tf_op | source)
XLA Modules:
  0.0 228.1 jit_solution(11906303229060757641)
XLA Ops:
  0.6 0.8 tile.9
  1.4 0.1 copy.9
  1.5 0.7 broadcast_in_dim.14.w_ref
  2.2 220.1 %corner_window.1 = (bf16[4096,256]{1,0:T(8,128)(2,1)}, f32[32,256]{1,0:T(8,128)}, bf16[32,512]{1,0:T(8,128)(2,1)}) custom-call(bf16[1024,8192]{1,0:T(8,128)(2,1)} %bitcast.17, bf16[4096,8192]{1,0:T(8,128)(2,1)} %bitcast.1.a_ref, bf16[1024,512]{1,0:T(8,128)(2,1)} %bitcast.18, bf16[1024,256]{1,0:T(8,128)(2,1)} %bitcast.19, bf16[512,256]{1,0:T(8,128)(2,1)} %bitcast.20, ...), custom_call_target="tpu_custom_call" | custom-call | flops 42949672960 | bytes 83886080 | tf_op jit(solution)/shard_map/corner_window/pallas_call | solution.py:298
  222.3 3.0 %copy.13 = bf16[1,4096,256]{2,1,0:T(8,128)(2,1)} copy(bf16[1,4096,256]{2,1,0:T(8,128)(2,1)} %bitcast.12) | data formatting | bytes 4194304
  225.3 1.4 copy.14
  226.7 1.4 copy.15
  (1 shorter events, 0.0 us)
